TPU v7x, 256 devices: a whole 4x4x8 slice. The times are simulated.
256 devices in a mesh: outer: 16 (over z, x_hi), lat: 4 (over y), lon: 4 (over x_lo, core).
Axes of the slice: x: 4 (x_hi: 2, x_lo: 2; x = x_hi * 2 + x_lo), y: 4, z: 8, core: 2. Of those that a mesh axis runs over, the one named last changes fastest.
Arguments:
- tokens: bfloat16 [384, 2, 48, 2048], P(('outer', 'lat'), None, 'lon'), may hold values from -6 to 6
- norm_gain: float32 [2048], replicated, may hold values from 0.4 to 1.6
- w_qkv: bfloat16 [2048, 3, 2048], P(None, None, 'outer'), may hold values from -20 to 20
- w_out: bfloat16 [2048, 2048], P('outer'), may hold values from -0.125 to 0.125
- grad_out: bfloat16 [384, 2, 48, 2048], P(('outer', 'lat'), None, 'lon'), may hold values from -6 to 6
Outputs:
- output: bfloat16 [384, 2, 48, 2048], P(('outer', 'lat'), None, 'lon')
- grad_tokens: bfloat16 [384, 2, 48, 2048], P(('outer', 'lat'), None, 'lon')
- grad_wqkv: float32 [2048, 3, 2048], P(None, None, 'outer')
- grad_wout: float32 [2048, 2048], P('outer')
- grad_gain: float32 [2048], replicated
All inputs are finite; a program needn't handle non-finite values.
Results may differ from a plain program's by a relative error of at most 0.023.
Values may be sent and summed in bfloat16 or wider, within the bound.
No kernel may reach another device: no remote copies, remote signals or barrier semaphores. Data moves between devices by JAX's collectives and lax.ppermute only.
A program may use at most 128 MiB of HBM per device.

v0:
```python
import jax
import jax.numpy as jnp
from jax import lax
from jax.sharding import PartitionSpec as P

D = 2048
HEAD = 64
LEV = 2
CLAT = 3
WLON = 12


epsilon = 1e-05


def from_behind(x, axis, by):
    count = lax.axis_size(axis)
    return lax.ppermute(x, axis, [(i, (i + by) % count) for i in range(count)])


def normalize(tokens):
    values_f = tokens.astype(jnp.float32)
    average = jnp.mean(values_f, -1, keepdims=True)
    centered = values_f - average
    inverse_std = lax.rsqrt(jnp.mean(centered * centered, -1, keepdims=True) + epsilon)
    return (centered * inverse_std, inverse_std)


def contract_rows(left, right):
    return lax.dot_general(
        left, right, (((0,), (0,)), ((), ())), preferred_element_type=jnp.float32
    )


def contract_cols(left, right):
    return lax.dot_general(
        left, right, (((1,), (1,)), ((), ())), preferred_element_type=jnp.float32
    )


def roll_left(tensor):
    offset = WLON // 2
    incoming = from_behind(tensor[:, :, :offset], "lon", -1)
    return jnp.concatenate([tensor[:, :, offset:], incoming], axis=2)


def roll_right(tensor):
    offset = WLON // 2
    incoming = from_behind(tensor[:, :, tensor.shape[2] - offset :], "lon", 1)
    return jnp.concatenate([incoming, tensor[:, :, : tensor.shape[2] - offset]], axis=2)


def rows_upward(tensor):
    incoming = from_behind(tensor[:CLAT], ("outer", "lat"), -1)
    return jnp.concatenate([tensor[CLAT:], incoming], axis=0)


def rows_downward(tensor):
    incoming = from_behind(tensor[tensor.shape[0] - CLAT :], ("outer", "lat"), 1)
    return jnp.concatenate([incoming, tensor[: tensor.shape[0] - CLAT]], axis=0)


def to_windows(flat, replicas, longitude):
    channels = flat.shape[-1]
    blocks = longitude // WLON
    shaped = flat.reshape(replicas, 2 * CLAT, LEV, blocks, WLON, channels).transpose(
        0, 3, 1, 2, 4, 5
    )
    return shaped.reshape(replicas * blocks, 2 * CLAT * LEV * WLON, channels)


def from_windows(windowed, replicas, longitude):
    channels = windowed.shape[-1]
    blocks = longitude // WLON
    shaped = windowed.reshape(replicas, blocks, 2 * CLAT, LEV, WLON, channels).transpose(
        0, 2, 3, 1, 4, 5
    )
    return shaped.reshape(replicas * 2 * CLAT * LEV * longitude, channels)


def shards(tokens, norm_gain, w_qkv, w_out, grad_out):
    replicas = lax.axis_size("outer")
    lat_count = lax.axis_size("lat")
    lat_index = lax.axis_index("lat")
    longitude = tokens.shape[2]
    blocks = longitude // WLON
    heads_dev = w_qkv.shape[2]
    head_count = heads_dev // HEAD
    score_scale = HEAD ** (-0.5)
    w_flat = w_qkv.reshape(D, 3 * heads_dev)
    standard, inverse_std = normalize(tokens)
    normed = (standard * norm_gain).astype(jnp.bfloat16)
    rolled = rows_upward(roll_left(normed))
    gathered = lax.all_gather(rolled, "outer", axis=0, tiled=True).reshape(-1, D)
    projected = jnp.dot(gathered, w_flat, preferred_element_type=jnp.float32).astype(jnp.bfloat16)
    windows = to_windows(projected, replicas, longitude)
    window_count = windows.shape[0]
    window_size = windows.shape[1]
    queries = windows[:, :, :heads_dev].reshape(window_count, window_size, head_count, HEAD)
    keys_all = windows[:, :, heads_dev : 2 * heads_dev].reshape(
        window_count, window_size, head_count, HEAD
    )
    values = windows[:, :, 2 * heads_dev :].reshape(window_count, window_size, head_count, HEAD)
    band_index = jnp.arange(replicas)
    cut_band = jnp.logical_and(lat_index == lat_count - 1, band_index == replicas - 1)
    cut_window = jnp.repeat(cut_band, blocks)
    half_index = jnp.arange(window_size) // (CLAT * LEV * WLON)
    same_half = half_index[:, None] == half_index[None, :]
    allowed = jnp.logical_or(jnp.logical_not(cut_window)[:, None, None], same_half[None])
    scores = (
        jnp.einsum("wqhd,wkhd->whqk", queries, keys_all, preferred_element_type=jnp.float32)
        * score_scale
    )
    scores = jnp.where(allowed[:, None], scores, -1e30)
    largest = jnp.max(scores, -1, keepdims=True)
    exponent = jnp.exp(scores - largest)
    softmax_weights = exponent / jnp.sum(exponent, -1, keepdims=True)
    weights_low = softmax_weights.astype(jnp.bfloat16)
    attended = jnp.einsum(
        "whqk,wkhd->wqhd", weights_low, values, preferred_element_type=jnp.float32
    )
    attended = attended.astype(jnp.bfloat16).reshape(window_count, window_size, heads_dev)
    attended_flat = from_windows(attended, replicas, longitude)
    picked = attended_flat
    branch = lax.psum_scatter(
        jnp.dot(picked, w_out, preferred_element_type=jnp.float32).astype(jnp.bfloat16),
        "outer",
        scatter_dimension=0,
        tiled=True,
    )
    branch_low = roll_right(rows_downward(branch.reshape(tokens.shape)))
    output = (tokens.astype(jnp.float32) + branch_low.astype(jnp.float32)).astype(jnp.bfloat16)
    cotangent = rows_upward(roll_left(grad_out))
    cot_all = lax.all_gather(cotangent, "outer", axis=0, tiled=True).reshape(-1, D)
    grad_wout = contract_rows(attended_flat, cot_all)
    d_attended = contract_cols(cot_all, w_out).astype(jnp.bfloat16)
    d_window = to_windows(d_attended, replicas, longitude).reshape(
        window_count, window_size, head_count, HEAD
    )
    d_weights = jnp.einsum("wqhd,wkhd->whqk", d_window, values, preferred_element_type=jnp.float32)
    row_dots = jnp.sum(softmax_weights * d_weights, -1, keepdims=True)
    d_scores = (softmax_weights * (d_weights - row_dots) * score_scale).astype(jnp.bfloat16)
    d_query = jnp.einsum("whqk,wkhd->wqhd", d_scores, keys_all, preferred_element_type=jnp.float32)
    d_key = jnp.einsum("whqk,wqhd->wkhd", d_scores, queries, preferred_element_type=jnp.float32)
    d_value = jnp.einsum(
        "whqk,wqhd->wkhd", weights_low, d_window, preferred_element_type=jnp.float32
    )
    d_projected = jnp.concatenate(
        [
            d_query.reshape(window_count, window_size, heads_dev),
            d_key.reshape(window_count, window_size, heads_dev),
            d_value.reshape(window_count, window_size, heads_dev),
        ],
        axis=-1,
    )
    d_flat = from_windows(d_projected.astype(jnp.bfloat16), replicas, longitude)
    grad_wqkv = contract_rows(gathered, d_flat)
    picked = d_flat
    d_rolled = lax.psum_scatter(
        contract_cols(picked, w_flat).astype(jnp.bfloat16), "outer", scatter_dimension=0, tiled=True
    )
    d_normed = roll_right(rows_downward(d_rolled.reshape(tokens.shape))).astype(jnp.float32)
    gain_local = jnp.sum((d_normed * standard).reshape(-1, D), 0)
    scaled = d_normed * norm_gain
    d_local = inverse_std * (
        scaled
        - jnp.mean(scaled, -1, keepdims=True)
        - standard * jnp.mean(scaled * standard, -1, keepdims=True)
    )
    grad_tokens = (grad_out.astype(jnp.float32) + d_local).astype(jnp.bfloat16)
    grad_wqkv, grad_wout = (
        lax.psum(grad_wqkv.astype(jnp.bfloat16), ("lat", "lon")).astype(jnp.float32),
        lax.psum(grad_wout.astype(jnp.bfloat16), ("lat", "lon")).astype(jnp.float32),
    )
    grad_gain = lax.psum(gain_local, ("outer", "lat", "lon"))
    return (output, grad_tokens, grad_wqkv.reshape(D, 3, heads_dev), grad_wout, grad_gain)


def solution(mesh):
    in_specs = (
        P(("outer", "lat"), None, "lon", None),
        P(),
        P(None, None, "outer"),
        P("outer", None),
        P(("outer", "lat"), None, "lon", None),
    )
    out_specs = (
        P(("outer", "lat"), None, "lon", None),
        P(("outer", "lat"), None, "lon", None),
        P(None, None, "outer"),
        P("outer", None),
        P(),
    )
    return jax.shard_map(shards, mesh=mesh, in_specs=in_specs, out_specs=out_specs, check_vma=False)
```

profile of v0, /device:TPU:1, one launch (start us, length us, event | category | flops | bytes accessed | tf_op | source)
XLA Modules:
  0.0 1140.5 jit_solution(4722600424669560236)
XLA Ops:
  20.3 10.5 collective-permute-start.1
  30.8 8.9 collective-permute-done.1
  42.0 6.0 collective-permute-done.4
  48.8 7.8 collective-permute-start.5
  56.6 10.3 collective-permute-done.5
  71.6 117.6 %all-gather.3.cloned.1.call-done = bf16[96,2,12,2048]{3,1,2,0:T(2,128)(2,1)} async-done(((bf16[6,2,12,2048]{3,1,2,0:T(2,128)(2,1)}), bf16[96,2,12,2048]{3,1,2,0:T(2,128)(2,1)}) %all-gather.3.cloned.1.call-update) | async-done | bytes 9437200 | tf_op jit(solution)/shard_map/all_gather | solution.py:94
  189.3 11.8 %copy.47 = bf16[96,2,12,2048]{3,2,1,0:T(8,128)(2,1)} copy(bf16[96,2,12,2048]{3,1,2,0:T(2,128)(2,1)} %all-gather.3.cloned.1.call-done) | data formatting | bytes 18874368 | tf_op jit(solution)/shard_map/all_gather | solution.py:94
  201.0 15.6 %reshape.137 = bf16[2304,2048]{1,0:T(8,128)(2,1)} reshape(bf16[96,2,12,2048]{3,2,1,0:T(8,128)(2,1)} %copy.47) | data formatting | bytes 18874368 | tf_op jit(solution)/shard_map/reshape | solution.py:94
  216.6 7.9 convolution_convert_fusion.2
  227.8 107.7 %all-gather.5.cloned.1.call-done = bf16[96,2,12,2048]{3,1,2,0:T(2,128)(2,1)} async-done(((bf16[6,2,12,2048]{3,1,2,0:T(2,128)(2,1)}), bf16[96,2,12,2048]{3,1,2,0:T(2,128)(2,1)}) %all-gather.5.cloned.1.call-update) | async-done | bytes 9437200 | tf_op jit(solution)/shard_map/all_gather | solution.py:134
  335.6 11.8 %copy.55 = bf16[96,2,12,2048]{3,2,1,0:T(8,128)(2,1)} copy(bf16[96,2,12,2048]{3,1,2,0:T(2,128)(2,1)} %all-gather.5.cloned.1.call-done) | data formatting | bytes 18874368 | tf_op jit(solution)/shard_map/all_gather | solution.py:134
  347.3 15.3 %reshape.142 = bf16[2304,2048]{1,0:T(8,128)(2,1)} reshape(bf16[96,2,12,2048]{3,2,1,0:T(8,128)(2,1)} %copy.55) | data formatting | bytes 18874368 | tf_op jit(solution)/shard_map/reshape | solution.py:134
  362.7 6.3 convolution_convert_fusion.3
  371.8 5.8 fusion.66
  386.5 9.5 fusion.42
  396.0 9.1 fusion.39
  410.8 6.4 convolution_convert_fusion.5
  424.9 9.2 convolution_convert_fusion.4
  436.9 9.0 convolution_convert_fusion
  451.1 112.7 %all-reduce.3.cloned.1.call-done = (bf16[2048,3,128]{2,0,1:T(8,128)(2,1)}, bf16[128,2048]{1,0:T(8,128)(2,1)}) async-done(((bf16[2048,3,128]{2,0,1:T(8,128)(2,1)}, bf16[128,2048]{1,0:T(8,128)(2,1)}), (bf16[2048,3,128]{2,0,1:T(8,128)(2,1)}, bf16[128,2048]{1,0:T(8,128)(2,1)})) %all-reduce.3.cloned.1.call-update) | async-done | bytes 2097168 | tf_op jit(solution)/shard_map/psum | solution.py:172
  567.9 229.4 %reduce-scatter.5.cloned.1.call-done = bf16[144,2048]{1,0:T(8,128)(2,1)} async-done(((bf16[2304,2048]{1,0:T(8,128)(2,1)}), bf16[144,2048]{1,0:T(8,128)(2,1)}) %reduce-scatter.5.cloned.1.call-update) | async-done | bytes 589840 | tf_op jit(solution)/shard_map/reduce_scatter | solution.py:159
  800.1 232.3 %reduce-scatter.3.cloned.1.call-done = bf16[144,2048]{1,0:T(8,128)(2,1)} async-done(((bf16[2304,2048]{1,0:T(8,128)(2,1)}), bf16[144,2048]{1,0:T(8,128)(2,1)}) %reduce-scatter.3.cloned.1.call-update) | async-done | bytes 589840 | tf_op jit(solution)/shard_map/reduce_scatter | solution.py:125
  1046.9 6.2 collective-permute-start.3
  1054.2 75.3 %psum.23 = f32[2048]{0:T(1024)} all-reduce(f32[2048]{0:T(1024)S(1)} %get-tuple-element.15), channel_id=1, replica_groups=mesh['outer'=16,'lat'=4,'lon'=4] {'outer','lat','lon'}, use_global_device_ids=true, to_apply=%region_12.13 | all-reduce | flops 2048 | bytes 16384 | tf_op jit(solution)/shard_map/psum | solution.py:175
  (108 shorter events, 83.8 us)
Async XLA Ops:
  7.2 355.5 %copy-start = (bf16[128,2048]{1,0:T(8,128)(2,1)S(1)}, bf16[128,2048]{1,0:T(8,128)(2,1)}, u32[]{:S(2)}) copy-start(bf16[128,2048]{1,0:T(8,128)(2,1)} %param.8) | copy-start | bytes 1572868
  7.2 182.1 %all-gather.3.cloned.1.call-start = ((), (), s32[]{:S(2)}) async-start(), calls=%async_computation.2 | async-start | bytes 10027008 | tf_op jit(solution)/shard_map/all_gather | solution.py:94
  11.9 8.1 collective-permute-start
  20.0 21.3 %copy-start.3 = (bf16[6,2,12,2048]{3,1,2,0:T(2,128)(2,1)S(1)}, bf16[6,2,12,2048]{3,1,2,0:T(2,128)(2,1)}, u32[]{:S(2)}) copy-start(bf16[6,2,12,2048]{3,1,2,0:T(2,128)(2,1)} %param.9) | copy-start | bytes 1769476
  20.3 19.4 %collective-permute-start.1 = (bf16[3,2,12,2048]{3,2,1,0:T(8,128)(2,1)S(1)}, bf16[3,2,12,2048]{3,2,1,0:T(8,128)(2,1)S(1)}, u32[]{:S(2)}, u32[]{:S(2)}) collective-permute-start(bf16[3,2,12,2048]{3,2,1,0:T(8,128)(2,1)S(1)} %get-tuple-element.28), channel_id=1, source_target_pairs={{0,252},{4,0},{8,4},{12,8},{16,12},{20,16},{24,20},{28,24},{32,28}... | collective-permute-start | bytes 884744 | tf_op jit(solution)/shard_map/ppermute | solution.py:18
  41.2 27.5 %copy-start.5 = (bf16[2048,3,128]{2,0,1:T(8,128)(2,1)S(1)}, bf16[2048,3,128]{2,0,1:T(8,128)(2,1)}, u32[]{:S(2)}) copy-start(bf16[2048,3,128]{2,0,1:T(8,128)(2,1)} %param.7) | copy-start | bytes 4718596
  41.2 294.3 %all-gather.5.cloned.1.call-start = ((), (), s32[]{:S(2)}) async-start(), calls=%async_computation.4 | async-start | bytes 10027008 | tf_op jit(solution)/shard_map/all_gather | solution.py:134
  41.8 6.2 collective-permute-start.4
  48.8 18.1 %collective-permute-start.5 = (bf16[3,2,12,2048]{3,1,2,0:T(2,128)(2,1)S(1)}, bf16[3,2,12,2048]{3,1,2,0:T(2,128)(2,1)S(1)}, u32[]{:S(2)}, u32[]{:S(2)}) collective-permute-start(bf16[3,2,12,2048]{3,1,2,0:T(2,128)(2,1)S(1)} %get-tuple-element.36), channel_id=1, source_target_pairs={{0,252},{4,0},{8,4},{12,8},{16,12},{20,16},{24,20},{28,24},{32,28}... | collective-permute-start | bytes 884744 | tf_op jit(solution)/shard_map/ppermute | solution.py:18
  68.4 495.4 %all-reduce.3.cloned.1.call-start = ((), (), s32[]{:S(2)}) async-start(), calls=%async_computation.6 | async-start | bytes 4194304 | tf_op jit(solution)/shard_map/psum | solution.py:172
  201.0 15.6 %copy-start.6 = (bf16[2048,3,128]{0,2,1:T(8,128)(2,1)S(1)}, bf16[2048,3,128]{0,2,1:T(8,128)(2,1)}, u32[]{:S(2)}) copy-start(bf16[2048,3,128]{0,2,1:T(8,128)(2,1)} %copy.48) | copy-start | bytes 4718596
  386.5 9.5 copy-start.9
  396.0 9.1 copy-start.11
  410.8 6.4 copy-start.10
  424.9 9.2 copy-start.12
  436.8 360.5 %reduce-scatter.5.cloned.1.call-start = ((), (), s32[]{:S(2)}) async-start(), calls=%async_computation.5 | async-start | bytes 10027008 | tf_op jit(solution)/shard_map/reduce_scatter | solution.py:159
  446.0 586.4 %reduce-scatter.3.cloned.1.call-start = ((), (), s32[]{:S(2)}) async-start(), calls=%async_computation.3 | async-start | bytes 10027008 | tf_op jit(solution)/shard_map/reduce_scatter | solution.py:125
  798.6 236.4 %collective-permute-start.6 = (bf16[3,2,12,2048]{3,2,1,0:T(8,128)(2,1)S(1)}, bf16[3,2,12,2048]{3,2,1,0:T(8,128)(2,1)S(1)}, u32[]{:S(2)}, u32[]{:S(2)}) collective-permute-start(bf16[3,2,12,2048]{3,2,1,0:T(8,128)(2,1)S(1)} %slice.87), channel_id=1, source_target_pairs={{0,4},{4,8},{8,12},{12,16},{16,20},{20,24},{24,28},{28,32},{32,36}... | collective-permute-start | bytes 884744 | tf_op jit(solution)/shard_map/ppermute | solution.py:18
  1033.6 12.4 %collective-permute-start.2 = (bf16[3,2,12,2048]{3,2,1,0:T(8,128)(2,1)S(1)}, bf16[3,2,12,2048]{3,2,1,0:T(8,128)(2,1)S(1)}, u32[]{:S(2)}, u32[]{:S(2)}) collective-permute-start(bf16[3,2,12,2048]{3,2,1,0:T(8,128)(2,1)S(1)} %slice.77), channel_id=1, source_target_pairs={{0,4},{4,8},{8,12},{12,16},{16,20},{20,24},{24,28},{28,32},{32,36}... | collective-permute-start | bytes 884744 | tf_op jit(solution)/shard_map/ppermute | solution.py:18
  1035.0 18.1 %copy-start.1 = (bf16[6,2,12,2048]{3,1,2,0:T(2,128)(2,1)S(1)}, bf16[6,2,12,2048]{3,1,2,0:T(2,128)(2,1)}, u32[]{:S(2)}) copy-start(bf16[6,2,12,2048]{3,1,2,0:T(2,128)(2,1)} %param.5) | copy-start | bytes 1769476
  1035.0 18.1 %copy-start.13 = (f32[2048]{0:T(1024)S(1)}, f32[2048]{0:T(1024)}, u32[]{:S(2)}) copy-start(f32[2048]{0:T(1024)} %param.6) | copy-start | bytes 24580
  1035.1 94.4 %copy-start.4 = (bf16[6,2,12,2048]{3,1,2,0:T(2,128)(2,1)S(1)}, bf16[6,2,12,2048]{3,1,2,0:T(2,128)(2,1)}, u32[]{:S(2)}) copy-start(bf16[6,2,12,2048]{3,1,2,0:T(2,128)(2,1)} %param.9) | copy-start | bytes 1769476
  1035.2 18.0 %collective-permute-start.7 = (bf16[6,2,6,2048]{3,2,1,0:T(8,128)(2,1)S(1)}, bf16[6,2,6,2048]{3,2,1,0:T(8,128)(2,1)S(1)}, u32[]{:S(2)}, u32[]{:S(2)}) collective-permute-start(bf16[6,2,6,2048]{3,2,1,0:T(8,128)(2,1)S(1)} %get-tuple-element.23), channel_id=1, source_target_pairs={{0,1},{1,2},{2,3},{3,0},{4,5},{5,6},{6,7},{7,4},{8,9},{9,10},{10,1... | collective-permute-start | bytes 884744 | tf_op jit(solution)/shard_map/ppermute | solution.py:18
  1046.9 82.6 %collective-permute-start.3 = (bf16[6,2,6,2048]{3,2,1,0:T(8,128)(2,1)}, bf16[6,2,6,2048]{3,2,1,0:T(8,128)(2,1)S(1)}, u32[]{:S(2)}, u32[]{:S(2)}) collective-permute-start(bf16[6,2,6,2048]{3,2,1,0:T(8,128)(2,1)} %get-tuple-element.25), channel_id=1, source_target_pairs={{0,1},{1,2},{2,3},{3,0},{4,5},{5,6},{6,7},{7,4},{8,9},{9,10},{10,1... | collective-permute-start | bytes 884744 | tf_op jit(solution)/shard_map/ppermute | solution.py:18
  (4 other events, 15.3 us)
Sparse Core Ops, SparseCore 0:
  41.3 147.8 all-gather.2
  192.4 143.0 all-gather.4
  437.0 126.7 all-reduce.2
  567.9 229.4 reduce-scatter.4
  802.0 230.2 reduce-scatter.2
where the time goes:
time: 1150 us; the launch traced here: 1140 us
  waiting for transfers between devices  835 us (73%)
  local copies, waits for them, and re-layouts  86.7 us (8%)
  matrix products  77.3 us (7%)
  blocking collectives  75.3 us (7%)
  starting transfers between devices  36.6 us (3%)
  other arithmetic  15.1 us (1%)
  between operations  14.3 us (1%)
    reduce_scatter x1, waiting for transfers between devices, shards(): lax.psum_scatter(jnp.dot(picked, w_out, preferred_element_type=jnp.float3...  232 us
    reduce_scatter x1, waiting for transfers between devices, shards(): lax.psum_scatter(contract_cols(picked, w_flat).astype(jnp.bfloat16), 'out...  229 us
    all_gather x1, waiting for transfers between devices, shards(): lax.all_gather(rolled, 'outer', axis=0, tiled=True).reshape(-1, D)  118 us
    psum x1, waiting for transfers between devices, shards(): lax.psum(grad_wqkv.astype(jnp.bfloat16), ('lat', 'lon')).astype(jnp.float32)  113 us
    all_gather x1, waiting for transfers between devices, shards(): lax.all_gather(cotangent, 'outer', axis=0, tiled=True).reshape(-1, D)  108 us
    psum x1, blocking collectives, shards(): grad_gain = lax.psum(gain_local, ('outer', 'lat', 'lon'))  75.3 us
    ppermute x8, starting transfers between devices, from_behind(): return lax.ppermute(x, axis, [(i, (i + by) % count) for i in range(count)])  36.2 us
    ppermute x8, waiting for transfers between devices, from_behind(): return lax.ppermute(x, axis, [(i, (i + by) % count) for i in range(count)])  35.5 us
  transfers between devices with their start and end apart: 13, of which 10 were waited for; matrix products, arithmetic and copies ran while one was open for 6% of the time, Pallas kernels for 0%

commit v1 on v0

v1 whole, which is shorter than its diff:
```python
import jax
import jax.numpy as jnp
from jax import lax
from jax.sharding import Mesh, PartitionSpec as P
from jax.experimental import pallas as pl
from jax.experimental.pallas import tpu as pltpu

D = 2048
HEAD = 64
LEV = 2
CLAT = 3
WLON = 12
WIN = 2 * CLAT * LEV * WLON
HALF = WIN // 2
SLOTS = 8
STEP = 2
ROWS = STEP * WIN
COLS = 256
HEADS_DEV = COLS // HEAD
SCALE = HEAD ** (-0.5)
BLK = 128
bf16 = jnp.bfloat16
f32 = jnp.float32


def nn(a, b):
    return lax.dot_general(a, b, (((1,), (0,)), ((), ())), preferred_element_type=f32)


def nt(a, b):
    return lax.dot_general(a, b, (((1,), (1,)), ((), ())), preferred_element_type=f32)


def tn(a, b):
    return lax.dot_general(a, b, (((0,), (0,)), ((), ())), preferred_element_type=f32)


def forward_kernel(cut_ref, x_ref, wg_ref, qkv_ref, att_ref, p_ref, own_ref, sib_ref, wq_ref, wo_ref):
    step = pl.program_id(0)

    @pl.when(step == 0)
    def _():
        for part in range(16):
            rows = slice(part * BLK, (part + 1) * BLK)
            for blk in range(2):
                for i in range(3):
                    wq_ref[rows, (2 * i + blk) * BLK : (2 * i + blk + 1) * BLK] = wg_ref[part, blk, i]
                wo_ref[blk * BLK : (blk + 1) * BLK, rows] = wg_ref[part, blk, 3]

    for n in range(3):
        cols = slice(n * COLS, (n + 1) * COLS)
        qkv_ref[:, cols] = nn(x_ref[...], wq_ref[:, cols]).astype(bf16)
    row = lax.broadcasted_iota(jnp.int32, (WIN, WIN), 0) >= HALF
    col = lax.broadcasted_iota(jnp.int32, (WIN, WIN), 1) >= HALF
    same = row == col
    for w in range(STEP):
        rows = slice(w * WIN, (w + 1) * WIN)
        allowed = jnp.logical_or(same, cut_ref[step * STEP + w] == 0)
        for h in range(HEADS_DEV):
            q = qkv_ref[rows, h * HEAD : (h + 1) * HEAD]
            k = qkv_ref[rows, COLS + h * HEAD : COLS + (h + 1) * HEAD]
            v = qkv_ref[rows, 2 * COLS + h * HEAD : 2 * COLS + (h + 1) * HEAD]
            s = jnp.where(allowed, nt(q, k) * SCALE, -1e30)
            e = jnp.exp(s - jnp.max(s, -1, keepdims=True))
            p = e / jnp.sum(e, -1, keepdims=True)
            p_ref[w, h] = p
            att_ref[rows, h * HEAD : (h + 1) * HEAD] = nn(p.astype(bf16), v).astype(bf16)

    def project(out_ref):
        for n in range(8):
            cols = slice(n * COLS, (n + 1) * COLS)
            out_ref[:, cols] = nn(att_ref[...], wo_ref[:, cols]).astype(bf16)

    @pl.when(step < SLOTS // STEP // 2)
    def _():
        project(own_ref)

    @pl.when(step >= SLOTS // STEP // 2)
    def _():
        project(sib_ref)


def backward_kernel(cot_ref, qkv_ref, p_ref, wq_ref, wo_ref, dp_ref, own_ref, sib_ref):
    step = pl.program_id(0)
    d_att = nt(cot_ref[...], wo_ref[...]).astype(bf16)
    for w in range(STEP):
        rows = slice(w * WIN, (w + 1) * WIN)
        for h in range(HEADS_DEV):
            hc = slice(h * HEAD, (h + 1) * HEAD)
            q = qkv_ref[rows, h * HEAD : (h + 1) * HEAD]
            k = qkv_ref[rows, COLS + h * HEAD : COLS + (h + 1) * HEAD]
            v = qkv_ref[rows, 2 * COLS + h * HEAD : 2 * COLS + (h + 1) * HEAD]
            p = p_ref[w, h]
            d_o = d_att[rows, hc]
            d_w = nt(d_o, v)
            dots = jnp.sum(p * d_w, -1, keepdims=True)
            d_s = (p * (d_w - dots) * SCALE).astype(bf16)
            dp_ref[rows, h * HEAD : (h + 1) * HEAD] = nn(d_s, k).astype(bf16)
            dp_ref[rows, COLS + h * HEAD : COLS + (h + 1) * HEAD] = tn(d_s, q).astype(bf16)
            dp_ref[rows, 2 * COLS + h * HEAD : 2 * COLS + (h + 1) * HEAD] = tn(p.astype(bf16), d_o).astype(bf16)

    def project(out_ref):
        for n in range(8):
            cols = slice(n * COLS, (n + 1) * COLS)
            out_ref[:, cols] = nt(dp_ref[...], wq_ref[cols, :]).astype(bf16)

    @pl.when(step < SLOTS // STEP // 2)
    def _():
        project(own_ref)

    @pl.when(step >= SLOTS // STEP // 2)
    def _():
        project(sib_ref)


def grads_kernel(x_ref, cot_ref, dp_ref, att_ref, g_ref):
    gq = tn(x_ref[...], dp_ref[...]).astype(bf16)
    go = tn(att_ref[...], cot_ref[...]).astype(bf16)
    for part in range(2):
        rows = slice(part * BLK, (part + 1) * BLK)
        for blk in range(2):
            for i in range(3):
                g_ref[part, blk, i] = gq[rows, (2 * i + blk) * BLK : (2 * i + blk + 1) * BLK]
            g_ref[part, blk, 3] = go[blk * BLK : (blk + 1) * BLK, rows]


def params():
    return pltpu.CompilerParams(dimension_semantics=("arbitrary",), vmem_limit_bytes=56 * 1024 * 1024)


HALF_STEPS = SLOTS // STEP // 2
own_spec = pl.BlockSpec((ROWS, D), lambda i: (jnp.minimum(i, HALF_STEPS - 1), 0))
sib_spec = pl.BlockSpec((ROWS, D), lambda i: (jnp.maximum(i - HALF_STEPS, 0), 0))


def rows_spec(cols):
    return pl.BlockSpec((ROWS, cols), lambda i: (i, 0))


def whole(*shape):
    return pl.BlockSpec(shape, lambda i: (0,) * len(shape))


def cost(flops, nbytes, exps=0):
    return pl.CostEstimate(flops=flops, bytes_accessed=nbytes, transcendentals=exps)


def shaped(shape, dtype=bf16):
    return jax.ShapeDtypeStruct(shape, dtype)


TOK = SLOTS * WIN


def forward(cut, x, wg):
    return pl.pallas_call(
        forward_kernel,
        grid=(SLOTS // STEP,),
        in_specs=[
            pl.BlockSpec(memory_space=pltpu.SMEM),
            rows_spec(D),
            whole(16, 2, 4, BLK, BLK),
        ],
        out_specs=[
            rows_spec(3 * COLS),
            rows_spec(COLS),
            pl.BlockSpec((STEP, HEADS_DEV, WIN, WIN), lambda i: (i, 0, 0, 0)),
            own_spec,
            sib_spec,
            whole(D, 3 * COLS),
            whole(COLS, D),
        ],
        out_shape=[
            shaped((TOK, 3 * COLS)),
            shaped((TOK, COLS)),
            shaped((SLOTS, HEADS_DEV, WIN, WIN), f32),
            shaped((TOK // 2, D)),
            shaped((TOK // 2, D)),
            shaped((D, 3 * COLS)),
            shaped((COLS, D)),
        ],
        compiler_params=params(),
        cost_estimate=cost(2 * TOK * D * 4 * COLS, 25 << 20, SLOTS * HEADS_DEV * WIN * WIN),
        name="attention_forward",
    )(cut, x, wg)


def backward(cot, qkv, p, wq, wo):
    return pl.pallas_call(
        backward_kernel,
        grid=(SLOTS // STEP,),
        in_specs=[
            rows_spec(D),
            rows_spec(3 * COLS),
            pl.BlockSpec((STEP, HEADS_DEV, WIN, WIN), lambda i: (i, 0, 0, 0)),
            whole(D, 3 * COLS),
            whole(COLS, D),
        ],
        out_specs=[rows_spec(3 * COLS), own_spec, sib_spec],
        out_shape=[shaped((TOK, 3 * COLS)), shaped((TOK // 2, D)), shaped((TOK // 2, D))],
        compiler_params=params(),
        cost_estimate=cost(2 * TOK * D * 4 * COLS, 25 << 20),
        name="attention_backward",
    )(cot, qkv, p, wq, wo)


def grads(x, cot, dp, att):
    return pl.pallas_call(
        grads_kernel,
        grid=(8,),
        in_specs=[
            pl.BlockSpec((TOK, 2 * BLK), lambda i: (0, i)),
            pl.BlockSpec((TOK, 2 * BLK), lambda i: (0, i)),
            whole(TOK, 3 * COLS),
            whole(TOK, COLS),
        ],
        out_specs=pl.BlockSpec((2, 2, 4, BLK, BLK), lambda i: (i, 0, 0, 0, 0)),
        out_shape=shaped((16, 2, 4, BLK, BLK)),
        compiler_params=params(),
        cost_estimate=cost(2 * TOK * D * 4 * COLS, 16 << 20),
        name="weight_gradients",
    )(x, cot, dp, att)


ALL = ("zh", "zl", "xh", "lat", "xl", "core")
OUTER = ("zh", "zl", "xh")
ROW = ("zh", "zl", "xh", "lat")
LON = ("xl", "core")
NEAR = ("zl", "xh")
PLANE = ("lat", "xl", "core")
EPSILON = 1e-05


def shift(x, axes, by):
    count = lax.axis_size(axes)
    return lax.ppermute(x, axes, [(i, (i + by) % count) for i in range(count)])


def swap(x, axes, mask):
    count = lax.axis_size(axes)
    return lax.ppermute(x, axes, [(i, i ^ mask) for i in range(count)])


def shift_both(x, by):
    rows, cols = lax.axis_size(ROW), lax.axis_size(LON)
    pairs = [
        (r * cols + c, (r + by) % rows * cols + (c + by) % cols)
        for r in range(rows)
        for c in range(cols)
    ]
    return lax.ppermute(x, ALL, pairs)


def roll_in(x):
    lon = WLON // 2
    corner = shift_both(x[:CLAT, :, :lon], -1)
    below = shift(x[:CLAT, :, lon:], ROW, -1)
    right = shift(x[CLAT:, :, :lon], LON, -1)
    top = jnp.concatenate([x[CLAT:, :, lon:], right], axis=2)
    bottom = jnp.concatenate([below, corner], axis=2)
    return jnp.concatenate([top, bottom], axis=0).reshape(WIN, D)


def roll_out(x):
    x = x.reshape(2 * CLAT, LEV, WLON, D)
    lon = WLON // 2
    corner = shift_both(x[CLAT:, :, lon:], 1)
    above = shift(x[CLAT:, :, :lon], ROW, 1)
    left = shift(x[:CLAT, :, lon:], LON, 1)
    top = jnp.concatenate([corner, above], axis=2)
    bottom = jnp.concatenate([left, x[:CLAT, :, :lon]], axis=2)
    return jnp.concatenate([top, bottom], axis=0)


def normalize(tokens):
    values = tokens.astype(f32)
    average = jnp.mean(values, -1, keepdims=True)
    centered = values - average
    inverse_std = lax.rsqrt(jnp.mean(centered * centered, -1, keepdims=True) + EPSILON)
    return centered * inverse_std, inverse_std


def share(x):
    mine = [x] + [swap(x, NEAR, s) for s in (1, 2, 3)]
    theirs = [swap(part, "core", 1) for part in mine]
    return jnp.concatenate(mine + theirs, axis=0)


def collect(own, sib):
    own = own.reshape(4, WIN, D)
    sib = sib.reshape(4, WIN, D)
    sums = {}
    for s in (3, 2, 1, 0):
        sums[s] = own[s].astype(f32) + swap(sib[s], "core", 1).astype(f32)
    total = sums[0]
    for s in (3, 2, 1):
        total = total + swap(sums[s].astype(bf16), NEAR, s).astype(f32)
    return total.astype(bf16)


def gather_weights(w_qkv, w_out):
    part = lax.axis_index(PLANE) * BLK
    qkv = lax.dynamic_slice(w_qkv, (part, 0, 0), (BLK, 3, BLK)).transpose(1, 0, 2)
    out = lax.dynamic_slice(w_out, (0, part), (BLK, BLK))
    unit = jnp.concatenate([qkv, out[None]], axis=0)
    blocks = lax.all_gather(unit, "zh", axis=0)
    mine = lax.all_to_all(blocks, "core", 0, 0, tiled=True)
    return lax.all_gather(mine.reshape(2, 2, 4, BLK, BLK), ("lat", "xl"), axis=0, tiled=True)


def reduce_weights(g):
    part = lax.psum_scatter(g, ("lat", "xl"), scatter_dimension=0, tiled=True)
    blocks = lax.all_to_all(part.reshape(4, 4, BLK, BLK), "core", 0, 0, tiled=True)
    unit = lax.psum_scatter(blocks, "zh", scatter_dimension=0, tiled=False)
    whole_block = lax.all_gather(unit, PLANE, axis=0)
    grad_qkv = whole_block[:, :3].transpose(0, 2, 1, 3).reshape(D, 3, BLK).astype(f32)
    grad_out = whole_block[:, 3].transpose(1, 0, 2).reshape(BLK, D).astype(f32)
    return grad_qkv, grad_out


def shards(tokens, norm_gain, w_qkv, w_out, grad_out):
    wg = gather_weights(w_qkv, w_out)
    rolled = roll_in(tokens)
    standard, inverse_std = normalize(rolled)
    normed = (standard * norm_gain).astype(bf16)
    x = share(normed)
    cotangent = roll_in(grad_out)
    cot = share(cotangent)

    near = lax.axis_index(NEAR)
    edge = jnp.logical_and(lax.axis_index("zh") == 3, lax.axis_index("lat") == 3)
    owners = near ^ (jnp.arange(SLOTS) % 4)
    cut = jnp.logical_and(edge, owners == 3).astype(jnp.int32)

    qkv, att, p, own, sib, wq, wo = forward(cut, x, wg)
    branch = collect(own, sib)
    output = roll_out((rolled.astype(f32) + branch.astype(f32)).astype(bf16))

    dp, d_own, d_sib = backward(cot, qkv, p, wq, wo)
    g = grads(x, cot, dp, att)
    grad_wqkv, grad_wout = reduce_weights(g)

    d_normed = collect(d_own, d_sib).astype(f32)
    gain_sum = jnp.sum(d_normed * standard, 0).reshape(16, BLK)
    for bit in range(8):
        gain_sum = gain_sum + swap(gain_sum, ALL, 1 << bit)
    scaled = d_normed * norm_gain
    d_local = inverse_std * (
        scaled
        - jnp.mean(scaled, -1, keepdims=True)
        - standard * jnp.mean(scaled * standard, -1, keepdims=True)
    )
    grad_tokens = roll_out((cotangent.astype(f32) + d_local).astype(bf16))
    return output, grad_tokens, grad_wqkv, grad_wout, gain_sum.reshape(D)


def solution(mesh):
    fine = Mesh(mesh.devices.reshape(4, 2, 2, 4, 2, 2), ALL)
    by_token = P(ROW, None, LON, None)
    in_specs = (by_token, P(), P(None, None, OUTER), P(OUTER, None), by_token)
    out_specs = (by_token, by_token, P(None, None, OUTER), P(OUTER, None), P())
    return jax.shard_map(shards, mesh=fine, in_specs=in_specs, out_specs=out_specs, check_vma=False)
```

time: 1150 us -> 498 us (0.43)
  waiting for transfers between devices: 835 us -> 278 us
  matrix products: 77.3 us -> 0 us
  Pallas kernels: 0 us -> 61.8 us
  local copies, waits for them, and re-layouts: 86.7 us -> 26.3 us
  blocking collectives: 75.3 us -> 32.7 us
  starting transfers between devices: 36.6 us -> 55.4 us
    reduce_scatter x2, waiting for transfers between devices: 462 us -> 86.8 us  [the longest x1 86.7 us: reduce_weights(): part = lax.psum_scatter(g, ('lat', 'xl'), scatter_dimension=0, tiled=True)]
    all_gather x2, waiting for transfers between devices: 225 us -> 30.9 us  [the longest x1 30.9 us: gather_weights(): lax.all_gather(mine.reshape(2, 2, 4, BLK, BLK), ('lat', 'xl'), axis=0, ti...]
    ppermute x8 -> x48, waiting for transfers between devices: 35.5 us -> 161 us  [the longest x36 128 us: swap(): return lax.ppermute(x, axes, [(i, i ^ mask) for i in range(count)])]
    psum x1 -> x0, waiting for transfers between devices: 113 us -> none  [shards(): lax.psum(grad_wqkv.astype(jnp.bfloat16), ('lat', 'lon')).astype(jnp.float32)]
    psum x1 -> x0, blocking collectives: 75.3 us -> none  [shards(): grad_gain = lax.psum(gain_local, ('outer', 'lat', 'lon'))]
    dot_general x11 -> x0, matrix products: 71.4 us -> none  [the longest x2 15.6 us: contract_rows(): lax.dot_general(left, right, (((0,), (0,)), ((), ())), preferred_element_...]
    pallas_call x0 -> x3, Pallas kernels: none -> 61.8 us  [the longest x1 25.3 us: forward(): pl.pallas_call(forward_kernel, grid=(SLOTS // STEP,), in_specs=[pl.BlockS...]
    reshape x3, local copies, waits for them, and re-layouts: 33.7 us -> 1.48 us  [the longest x2 1.34 us: roll_out(): x = x.reshape(2 * CLAT, LEV, WLON, D)]
  transfers between devices with their start and end apart: 13 -> 52, of which waited for: 10 -> 19; matrix products, arithmetic and copies ran while one was open for 6% -> 8% of each run, Pallas kernels for 0% -> 0%
where the time goes in v1:
time: 498 us; the launch traced here: 488 us
  waiting for transfers between devices  278 us (56%)
  Pallas kernels  61.8 us (12%)
  starting transfers between devices  55.4 us (11%)
  blocking collectives  32.7 us (7%)
  local copies, waits for them, and re-layouts  26.3 us (5%)
  other arithmetic  19.2 us (4%)
  between operations  14.7 us (3%)
    ppermute x36, waiting for transfers between devices, swap(): return lax.ppermute(x, axes, [(i, i ^ mask) for i in range(count)])  128 us
    reduce_scatter x1, waiting for transfers between devices, reduce_weights(): part = lax.psum_scatter(g, ('lat', 'xl'), scatter_dimension=0, tiled=True)  86.7 us
    ppermute x36, starting transfers between devices, swap(): return lax.ppermute(x, axes, [(i, i ^ mask) for i in range(count)])  32.8 us
    ppermute x8, waiting for transfers between devices, shift(): return lax.ppermute(x, axes, [(i, (i + by) % count) for i in range(count)])  30.9 us
    all_gather x1, waiting for transfers between devices, gather_weights(): lax.all_gather(mine.reshape(2, 2, 4, BLK, BLK), ('lat', 'xl'), axis=0, ti...  30.9 us
    pallas_call x1, Pallas kernels, forward(): pl.pallas_call(forward_kernel, grid=(SLOTS // STEP,), in_specs=[pl.BlockS...  25.3 us
    pallas_call x1, Pallas kernels, backward(): pl.pallas_call(backward_kernel, grid=(SLOTS // STEP,), in_specs=[rows_spe...  24.7 us
    all_gather x1, blocking collectives, gather_weights(): blocks = lax.all_gather(unit, 'zh', axis=0)  18.2 us
  transfers between devices with their start and end apart: 52, of which 19 were waited for; matrix products, arithmetic and copies ran while one was open for 8% of the time, Pallas kernels for 0%

profile of v1, /device:TPU:1, one launch (start us, length us, event | category | flops | bytes accessed | tf_op | source)
XLA Modules:
  0.0 488.5 jit_solution(8096511146185892432)
XLA Ops:
  8.6 18.2 %all-gather = bf16[16,128,128]{2,1,0:T(8,128)(2,1)S(1)} all-gather(bf16[4,128,128]{2,1,0:T(8,128)(2,1)S(1)} %pad_maximum_fusion), channel_id=2, replica_groups=mesh['zh'=4,'zl'=2,'xh'=2,'lat'=4,'xl'=2,'core'=2] {'zh'}, dimensions={0}, use_global_device_ids=true | all-gather | bytes 655360 | tf_op jit(solution)/shard_map/all_gather | solution.py:306
  26.8 8.1 %all_to_all.10 = bf16[4,4,128,128]{3,2,1,0:T(8,128)(2,1)} all-to-all(bf16[4,4,128,128]{3,2,1,0:T(8,128)(2,1)S(1)} %bitcast.24), channel_id=1, replica_groups=mesh['zh'=4,'zl'=2,'xh'=2,'lat'=4,'xl'=2,'core'=2] {'core'}, dimensions={0} | all-to-all | bytes 1048576 | tf_op jit(solution)/shard_map/all_to_all | solution.py:307
  35.9 7.4 %collective-permute-start.22 = (bf16[3,2,6,2048]{3,1,2,0:T(2,128)(2,1)S(1)}, bf16[3,2,6,2048]{3,1,2,0:T(2,128)(2,1)S(1)}, u32[]{:S(2)}, u32[]{:S(2)}) collective-permute-start(bf16[3,2,6,2048]{3,1,2,0:T(2,128)(2,1)S(1)} %get-tuple-element.79), channel_id=1, source_target_pairs={{0,255},{1,252},{2,253},{3,254},{4,3},{5,0},{6,1},{7,2},{8,7},{9,4... | collective-permute-start | bytes 442376 | tf_op jit(solution)/shard_map/ppermute | solution.py:251
  46.9 3.2 collective-permute-done.21
  51.5 20.8 %collective-permute-done = bf16[3,2,6,2048]{3,1,2,0:T(2,128)(2,1)S(1)} collective-permute-done((bf16[3,2,6,2048]{3,1,2,0:T(2,128)(2,1)S(1)}, bf16[3,2,6,2048]{3,1,2,0:T(2,128)(2,1)S(1)}, u32[]{:S(2)}, u32[]{:S(2)}) %collective-permute-start) | collective-permute-done | bytes 147488 | tf_op jit(solution)/shard_map/ppermute | solution.py:236
  77.3 24.5 %collective-permute-done.23 = bf16[144,2048]{1,0:T(8,128)(2,1)} collective-permute-done((bf16[144,2048]{1,0:T(8,128)(2,1)S(1)}, bf16[144,2048]{1,0:T(8,128)(2,1)}, u32[]{:S(2)}, u32[]{:S(2)}) %collective-permute-start.23) | collective-permute-done | bytes 589856 | tf_op jit(solution)/shard_map/ppermute | solution.py:241
  109.6 34.3 %collective-permute-done.3 = bf16[144,2048]{1,0:T(8,128)(2,1)S(1)} collective-permute-done((bf16[144,2048]{1,0:T(8,128)(2,1)S(1)}, bf16[144,2048]{1,0:T(8,128)(2,1)S(1)}, u32[]{:S(2)}, u32[]{:S(2)}) %collective-permute-start.3) | collective-permute-done | bytes 589856 | tf_op jit(solution)/shard_map/ppermute | solution.py:241
  155.2 30.9 %all-gather.4.cloned.1.call-done.wg_ref = bf16[16,2,4,128,128]{4,3,2,1,0:T(8,128)(2,1)} async-done(((bf16[2,2,4,128,128]{4,3,2,1,0:T(8,128)(2,1)}), bf16[16,2,4,128,128]{4,3,2,1,0:T(8,128)(2,1)}) %all-gather.4.cloned.1.call-update) | async-done | bytes 4194320 | tf_op jit(solution)/shard_map/all_gather | solution.py:308
  186.1 25.3 %attention_forward.1 = (bf16[1152,768]{1,0:T(8,128)(2,1)}, bf16[1152,256]{1,0:T(8,128)(2,1)}, f32[8,4,144,144]{3,2,1,0:T(8,128)}, bf16[576,2048]{1,0:T(8,128)(2,...) custom-call(s32[8]{0:T(128)} %and_convert_fusion.cut_ref, ...), custom_call_target="tpu_custom_call" | custom-call | flops 4831838208 | bytes 26214400 | tf_op jit(solution)/shard_map/attention_forward/pallas_call | solution.py:156
  211.4 24.7 %attention_backward.1 = (bf16[1152,768]{1,0:T(8,128)(2,1)}, bf16[576,2048]{1,0:T(8,128)(2,1)}, bf16[576,2048]{1,0:T(8,128)(2,1)}) custom-call(bf16[1152,2048]{1,0:T(8,128)(2,1)} %copy-done.7, bf16[1152,768]{1,0:T(8,128)(2,1)} %get-tuple-element.17.qkv_ref, f32[8,4,144,144]{3,2,1,0:T(8,128)} %get-tuple-element.18.p_ref, ...), custom_call_target="tpu_custom_call" | custom-call | flops 4831838208 | bytes 26214400 | tf_op jit(solution)/shard_map/attention_backward/pallas_call | solution.py:189
  236.1 11.8 %weight_gradients.1 = bf16[16,2,4,128,128]{4,3,2,1,0:T(8,128)(2,1)} custom-call(bf16[1152,2048]{1,0:T(8,128)(2,1)} %constant_dynamic-update-slice_fusion.x_ref, bf16[1152,2048]{1,0:T(8,128)(2,1)} %copy-done.7, bf16[1152,768]{1,0:T(8,128)(2,1)} %get-tuple-element.23.dp_ref, bf16[1152,256]{1,0:T(8,128)(2,1)} %get-tuple-element.24.att_ref), custom_call_target="tpu_custom_call" | custom-call | flops 4831838208 | bytes 16777216 | tf_op jit(solution)/shard_map/weight_gradients/pallas_call | solution.py:208
  251.9 86.7 %reduce-scatter.3.cloned.1.call-done = bf16[2,2,4,128,128]{4,3,2,1,0:T(8,128)(2,1)} async-done(((bf16[16,2,4,128,128]{4,3,2,1,0:T(8,128)(2,1)}), bf16[2,2,4,128,128]{4,3,2,1,0:T(8,128)(2,1)}) %reduce-scatter.3.cloned.1.call-update) | async-done | bytes 524304 | tf_op jit(solution)/shard_map/reduce_scatter | solution.py:312
  338.6 6.5 %all_to_all.11 = bf16[4,4,128,128]{3,2,1,0:T(8,128)(2,1)} all-to-all(bf16[4,4,128,128]{3,2,1,0:T(8,128)(2,1)} %bitcast.26), channel_id=1, replica_groups=mesh['zh'=4,'zl'=2,'xh'=2,'lat'=4,'xl'=2,'core'=2] {'core'}, dimensions={0} | all-to-all | bytes 1048576 | tf_op jit(solution)/shard_map/all_to_all | solution.py:313
  345.5 3.8 add_convert_fusion.3
  349.2 3.4 collective-permute-start.32
  355.9 17.6 %collective-permute-done.32 = bf16[144,2048]{1,0:T(8,128)(2,1)} collective-permute-done((bf16[144,2048]{1,0:T(8,128)(2,1)S(1)}, bf16[144,2048]{1,0:T(8,128)(2,1)}, u32[]{:S(2)}, u32[]{:S(2)}) %collective-permute-start.32) | collective-permute-done | bytes 589856 | tf_op jit(solution)/shard_map/ppermute | solution.py:241
  376.5 3.2 collective-permute-done.36
  380.1 7.0 %collective-permute-done.34 = bf16[144,2048]{1,0:T(8,128)(2,1)} collective-permute-done((bf16[144,2048]{1,0:T(8,128)(2,1)}, bf16[144,2048]{1,0:T(8,128)(2,1)}, u32[]{:S(2)}, u32[]{:S(2)}) %collective-permute-start.34) | collective-permute-done | bytes 589856 | tf_op jit(solution)/shard_map/ppermute | solution.py:241
  397.5 31.1 %collective-permute-done.41 = f32[16,128]{1,0:T(8,128)S(1)} collective-permute-done((f32[16,128]{1,0:T(8,128)S(1)}, f32[16,128]{1,0:T(8,128)S(1)}, u32[]{:S(2)}, u32[]{:S(2)}) %collective-permute-start.41) | collective-permute-done | bytes 8224 | tf_op jit(solution)/shard_map/ppermute | solution.py:241
  432.0 3.1 collective-permute-done.43
  446.2 4.5 collective-permute-start.37
  463.1 3.8 collective-permute-done.38
  470.4 3.1 collective-permute-done.18
  478.1 3.4 copy_convert_fusion
  (169 shorter events, 87.3 us)
Async XLA Ops:
  7.2 178.9 %all-gather.4.cloned.1.call-start = ((), (), s32[]{:S(2)}) async-start(), calls=%async_computation.4 | async-start | bytes 4718592 | tf_op jit(solution)/shard_map/all_gather | solution.py:308
  34.9 303.7 %reduce-scatter.3.cloned.1.call-start = ((), (), s32[]{:S(2)}) async-start(), calls=%async_computation.5 | async-start | bytes 4718592 | tf_op jit(solution)/shard_map/reduce_scatter | solution.py:312
  51.3 96.5 %collective-permute-start.26 = (bf16[144,2048]{1,0:T(8,128)(2,1)S(1)}, bf16[144,2048]{1,0:T(8,128)(2,1)}, u32[]{:S(2)}, u32[]{:S(2)}) collective-permute-start(bf16[144,2048]{1,0:T(8,128)(2,1)S(1)} %reshape.121), channel_id=1, source_target_pairs={{0,1},{1,0},{2,3},{3,2},{4,5},{5,4},{6,7},{7,6},{8,9},{9,8},{10,11... | collective-permute-start | bytes 1769480 | tf_op jit(solution)/shard_map/ppermute | solution.py:241
  51.4 54.2 %collective-permute-start.25 = (bf16[144,2048]{1,0:T(8,128)(2,1)S(1)}, bf16[144,2048]{1,0:T(8,128)(2,1)}, u32[]{:S(2)}, u32[]{:S(2)}) collective-permute-start(bf16[144,2048]{1,0:T(8,128)(2,1)S(1)} %reshape.121), channel_id=1, source_target_pairs={{0,48},{16,32},{32,16},{48,0},{1,49},{17,33},{33,17},{49,1},{2,50}... | collective-permute-start | bytes 1769480 | tf_op jit(solution)/shard_map/ppermute | solution.py:241
  72.3 30.7 %collective-permute-start.24 = (bf16[144,2048]{1,0:T(8,128)(2,1)S(1)}, bf16[144,2048]{1,0:T(8,128)(2,1)}, u32[]{:S(2)}, u32[]{:S(2)}) collective-permute-start(bf16[144,2048]{1,0:T(8,128)(2,1)S(1)} %reshape.121), channel_id=1, source_target_pairs={{0,32},{16,48},{32,0},{48,16},{1,33},{17,49},{33,1},{49,17},{2,34}... | collective-permute-start | bytes 1769480 | tf_op jit(solution)/shard_map/ppermute | solution.py:241
  72.4 29.4 %collective-permute-start.23 = (bf16[144,2048]{1,0:T(8,128)(2,1)S(1)}, bf16[144,2048]{1,0:T(8,128)(2,1)}, u32[]{:S(2)}, u32[]{:S(2)}) collective-permute-start(bf16[144,2048]{1,0:T(8,128)(2,1)S(1)} %reshape.121), channel_id=1, source_target_pairs={{0,16},{16,0},{32,48},{48,32},{1,17},{17,1},{33,49},{49,33},{2,18}... | collective-permute-start | bytes 1769480 | tf_op jit(solution)/shard_map/ppermute | solution.py:241
  76.8 72.1 %collective-permute-start.6 = (bf16[144,2048]{1,0:T(8,128)(2,1)S(1)}, bf16[144,2048]{1,0:T(8,128)(2,1)S(1)}, u32[]{:S(2)}, u32[]{:S(2)}) collective-permute-start(bf16[144,2048]{1,0:T(8,128)(2,1)S(1)} %get-tuple-element.50), channel_id=1, source_target_pairs={{0,1},{1,0},{2,3},{3,2},{4,5},{5,4},{6,7},{7,6},{8,9},{9,8},{10,11... | collective-permute-start | bytes 1769480 | tf_op jit(solution)/shard_map/ppermute | solution.py:241
  101.9 42.0 %collective-permute-start.3 = (bf16[144,2048]{1,0:T(8,128)(2,1)S(1)}, bf16[144,2048]{1,0:T(8,128)(2,1)S(1)}, u32[]{:S(2)}, u32[]{:S(2)}) collective-permute-start(bf16[144,2048]{1,0:T(8,128)(2,1)S(1)} %get-tuple-element.50), channel_id=1, source_target_pairs={{0,16},{16,0},{32,48},{48,32},{1,17},{17,1},{33,49},{49,33},{2,18}... | collective-permute-start | bytes 1769480 | tf_op jit(solution)/shard_map/ppermute | solution.py:241
  103.0 42.6 %collective-permute-start.4 = (bf16[144,2048]{1,0:T(8,128)(2,1)S(1)}, bf16[144,2048]{1,0:T(8,128)(2,1)S(1)}, u32[]{:S(2)}, u32[]{:S(2)}) collective-permute-start(bf16[144,2048]{1,0:T(8,128)(2,1)S(1)} %get-tuple-element.50), channel_id=1, source_target_pairs={{0,32},{16,48},{32,0},{48,16},{1,33},{17,49},{33,1},{49,17},{2,34}... | collective-permute-start | bytes 1769480 | tf_op jit(solution)/shard_map/ppermute | solution.py:241
  105.6 40.8 %collective-permute-start.5 = (bf16[144,2048]{1,0:T(8,128)(2,1)S(1)}, bf16[144,2048]{1,0:T(8,128)(2,1)S(1)}, u32[]{:S(2)}, u32[]{:S(2)}) collective-permute-start(bf16[144,2048]{1,0:T(8,128)(2,1)S(1)} %get-tuple-element.50), channel_id=1, source_target_pairs={{0,48},{16,32},{32,16},{48,0},{1,49},{17,33},{33,17},{49,1},{2,50}... | collective-permute-start | bytes 1769480 | tf_op jit(solution)/shard_map/ppermute | solution.py:241
  248.0 128.5 %reduce-scatter.5.cloned.1.call-start = ((), (), s32[]{:S(2)}) async-start(), calls=%async_computation.6 | async-start | bytes 655360 | tf_op jit(solution)/shard_map/reduce_scatter | solution.py:314
  250.8 94.6 %collective-permute-start.35 = (bf16[144,2048]{1,0:T(8,128)(2,1)}, bf16[144,2048]{1,0:T(8,128)(2,1)}, u32[]{:S(2)}, u32[]{:S(2)}) collective-permute-start(bf16[144,2048]{1,0:T(8,128)(2,1)} %get-tuple-element.54), channel_id=1, source_target_pairs={{0,1},{1,0},{2,3},{3,2},{4,5},{5,4},{6,7},{7,6},{8,9},{9,8},{10,11... | collective-permute-start | bytes 1769480 | tf_op jit(solution)/shard_map/ppermute | solution.py:241
  251.3 94.1 %collective-permute-start.33 = (bf16[144,2048]{1,0:T(8,128)(2,1)}, bf16[144,2048]{1,0:T(8,128)(2,1)}, u32[]{:S(2)}, u32[]{:S(2)}) collective-permute-start(bf16[144,2048]{1,0:T(8,128)(2,1)} %get-tuple-element.55), channel_id=1, source_target_pairs={{0,1},{1,0},{2,3},{3,2},{4,5},{5,4},{6,7},{7,6},{8,9},{9,8},{10,11... | collective-permute-start | bytes 1769480 | tf_op jit(solution)/shard_map/ppermute | solution.py:241
  251.4 94.1 %collective-permute-start.31 = (bf16[144,2048]{1,0:T(8,128)(2,1)S(1)}, bf16[144,2048]{1,0:T(8,128)(2,1)}, u32[]{:S(2)}, u32[]{:S(2)}) collective-permute-start(bf16[144,2048]{1,0:T(8,128)(2,1)S(1)} %get-tuple-element.56), channel_id=1, source_target_pairs={{0,1},{1,0},{2,3},{3,2},{4,5},{5,4},{6,7},{7,6},{8,9},{9,8},{10,11... | collective-permute-start | bytes 1769480 | tf_op jit(solution)/shard_map/ppermute | solution.py:241
  251.8 104.1 %collective-permute-start.30 = (bf16[144,2048]{1,0:T(8,128)(2,1)S(1)}, bf16[144,2048]{1,0:T(8,128)(2,1)}, u32[]{:S(2)}, u32[]{:S(2)}) collective-permute-start(bf16[144,2048]{1,0:T(8,128)(2,1)S(1)} %get-tuple-element.53), channel_id=1, source_target_pairs={{0,1},{1,0},{2,3},{3,2},{4,5},{5,4},{6,7},{7,6},{8,9},{9,8},{10,11... | collective-permute-start | bytes 1769480 | tf_op jit(solution)/shard_map/ppermute | solution.py:241
  345.2 130.1 %all-gather.6.cloned.1.call-start = ((), (), s32[]{:S(2)}) async-start(), calls=%async_computation.7 | async-start | bytes 2228224 | tf_op jit(solution)/shard_map/all_gather | solution.py:315
  353.2 33.9 %collective-permute-start.34 = (bf16[144,2048]{1,0:T(8,128)(2,1)}, bf16[144,2048]{1,0:T(8,128)(2,1)}, u32[]{:S(2)}, u32[]{:S(2)}) collective-permute-start(bf16[144,2048]{1,0:T(8,128)(2,1)} %get-tuple-element.59), channel_id=1, source_target_pairs={{0,32},{16,48},{32,0},{48,16},{1,33},{17,49},{33,1},{49,17},{2,34}... | collective-permute-start | bytes 1769480 | tf_op jit(solution)/shard_map/ppermute | solution.py:241
  354.7 36.4 %collective-permute-start.15 = (bf16[144,2048]{1,0:T(8,128)(2,1)}, bf16[144,2048]{1,0:T(8,128)(2,1)}, u32[]{:S(2)}, u32[]{:S(2)}) collective-permute-start(bf16[144,2048]{1,0:T(8,128)(2,1)} %get-tuple-element.61), channel_id=1, source_target_pairs={{0,1},{1,0},{2,3},{3,2},{4,5},{5,4},{6,7},{7,6},{8,9},{9,8},{10,11... | collective-permute-start | bytes 1769480 | tf_op jit(solution)/shard_map/ppermute | solution.py:241
  355.9 35.2 %collective-permute-start.13 = (bf16[144,2048]{1,0:T(8,128)(2,1)}, bf16[144,2048]{1,0:T(8,128)(2,1)}, u32[]{:S(2)}, u32[]{:S(2)}) collective-permute-start(bf16[144,2048]{1,0:T(8,128)(2,1)} %get-tuple-element.62), channel_id=1, source_target_pairs={{0,1},{1,0},{2,3},{3,2},{4,5},{5,4},{6,7},{7,6},{8,9},{9,8},{10,11... | collective-permute-start | bytes 1769480 | tf_op jit(solution)/shard_map/ppermute | solution.py:241
  379.6 61.0 %collective-permute-start.10 = (bf16[144,2048]{1,0:T(8,128)(2,1)S(1)}, bf16[144,2048]{1,0:T(8,128)(2,1)S(1)}, u32[]{:S(2)}, u32[]{:S(2)}) collective-permute-start(bf16[144,2048]{1,0:T(8,128)(2,1)S(1)} %get-tuple-element.60), channel_id=1, source_target_pairs={{0,1},{1,0},{2,3},{3,2},{4,5},{5,4},{6,7},{7,6},{8,9},{9,8},{10,11... | collective-permute-start | bytes 1769480 | tf_op jit(solution)/shard_map/ppermute | solution.py:241
  393.2 47.4 %collective-permute-start.12 = (bf16[144,2048]{1,0:T(8,128)(2,1)S(1)}, bf16[144,2048]{1,0:T(8,128)(2,1)S(1)}, u32[]{:S(2)}, u32[]{:S(2)}) collective-permute-start(bf16[144,2048]{1,0:T(8,128)(2,1)S(1)} %get-tuple-element.64), channel_id=1, source_target_pairs={{0,48},{16,32},{32,16},{48,0},{1,49},{17,33},{33,17},{49,1},{2,50}... | collective-permute-start | bytes 1769480 | tf_op jit(solution)/shard_map/ppermute | solution.py:241
  394.8 45.9 %collective-permute-start.16 = (bf16[144,2048]{1,0:T(8,128)(2,1)S(1)}, bf16[144,2048]{1,0:T(8,128)(2,1)S(1)}, u32[]{:S(2)}, u32[]{:S(2)}) collective-permute-start(bf16[144,2048]{1,0:T(8,128)(2,1)S(1)} %get-tuple-element.65), channel_id=1, source_target_pairs={{0,16},{16,0},{32,48},{48,32},{1,17},{17,1},{33,49},{49,33},{2,18}... | collective-permute-start | bytes 1769480 | tf_op jit(solution)/shard_map/ppermute | solution.py:241
  397.2 43.4 %collective-permute-start.14 = (bf16[144,2048]{1,0:T(8,128)(2,1)S(1)}, bf16[144,2048]{1,0:T(8,128)(2,1)S(1)}, u32[]{:S(2)}, u32[]{:S(2)}) collective-permute-start(bf16[144,2048]{1,0:T(8,128)(2,1)S(1)} %get-tuple-element.66), channel_id=1, source_target_pairs={{0,32},{16,48},{32,0},{48,16},{1,33},{17,49},{33,1},{49,17},{2,34}... | collective-permute-start | bytes 1769480 | tf_op jit(solution)/shard_map/ppermute | solution.py:241
  397.5 31.1 %collective-permute-start.41 = (f32[16,128]{1,0:T(8,128)S(1)}, f32[16,128]{1,0:T(8,128)S(1)}, u32[]{:S(2)}, u32[]{:S(2)}) collective-permute-start(f32[16,128]{1,0:T(8,128)S(1)} %bitcast_add_fusion), channel_id=1, source_target_pairs={{0,2},{1,3},{2,0},{3,1},{4,6},{5,7},{6,4},{7,5},{8,10},{9,11},{10,... | collective-permute-start | bytes 24584 | tf_op jit(solution)/shard_map/ppermute | solution.py:241
  (36 other events, 420.9 us)
Sparse Core Ops, SparseCore 0:
  35.0 151.0 all-gather.3
  248.1 90.4 reduce-scatter.2
  345.3 29.6 reduce-scatter.4
  376.6 50.0 all-gather.5
